TPU v7x, 32 devices: a whole 2x2x4 slice. The times are simulated.
32 devices in a mesh: dp: 4 (over y, x), section: 2 (over core), tensor: 4 (over z).
Axes of the slice: x: 2, y: 2, z: 4, core: 2. Of those that a mesh axis runs over, the one named last changes fastest.
Arguments:
- fwd_state: bfloat16 [2, 512, 4096], P('section', ('dp', 'tensor')), may hold values from -6 to 6
- bwd_state: bfloat16 [2, 512, 4096], P('section', ('dp', 'tensor')), may hold values from -6 to 6
- stash: bfloat16 [2, 2, 512, 4096], P('section', None, ('dp', 'tensor')), may hold values from -6 to 6
- gains: bfloat16 [2, 2, 4096], P('section'), may hold values from 0.25 to 1.75
- w_query: bfloat16 [2, 2, 4096, 4096], P('section', None, 'dp', 'tensor'), may hold values from -0.09375 to 0.09375
- w_key: bfloat16 [2, 2, 4096, 1024], P('section', None, 'dp', 'tensor'), may hold values from -0.09375 to 0.09375
- w_value: bfloat16 [2, 2, 4096, 1024], P('section', None, 'dp', 'tensor'), may hold values from -0.09375 to 0.09375
- w_out: bfloat16 [2, 2, 4096, 4096], P('section', None, 'tensor', 'dp'), may hold values from -0.09375 to 0.09375
- fwd_segments: int32 [2, 4, 128], P(None, 'dp'), may hold values from 0 to 3, never falling along the last dimension, each value on 1 to 64 neighbouring positions
- bwd_segments: int32 [2, 4, 128], P(None, 'dp'), may hold values from 0 to 3, never falling along the last dimension, each value on 1 to 64 neighbouring positions
Outputs:
- fwd_out: bfloat16 [2, 512, 4096], P('section', ('dp', 'tensor'))
- bwd_out: bfloat16 [2, 512, 4096], P('section', ('dp', 'tensor'))
- gain_grad: float32 [2, 2, 4096], P('section')
Inputs may be any that keep to these rules, and one draw needn't show every extreme that they name: `fwd_segments`: in each replica's rows of each micro-batch the document ids never fall; each document has at most 64 rows and one has exactly that many. `bwd_segments`: in each replica's rows of each micro-batch the document ids never fall; each document has at most 64 rows and one has exactly that many.
All inputs are finite; a program needn't handle non-finite values.
Results may differ from a plain program's by a relative error of at most 0.02.
Values may be sent and summed in bfloat16 or wider, within the bound.
A program may use at most 192 MiB of HBM per device.

v0:
```python
import functools
import math

import jax
import jax.numpy as jnp
from jax import lax
from jax.experimental import pallas as pl
from jax.experimental.pallas import tpu as pltpu
from jax.sharding import PartitionSpec as P

HD = 128
TICKS = 2
ROPE_BASE = 1000000.0
MESH = pl.DeviceIdType.MESH
F32 = jnp.float32
BF16 = jnp.bfloat16

WIDE = ("out", "all")


def exchange_kernel(kinds, n_dp, n_tensor, *refs):
    count = len(kinds)
    sources, targets = refs[:count], refs[count : 2 * count]
    send_sem, recv_sem, up_sem, down_sem, local_sem = refs[2 * count :]
    my_dp, my_tensor = lax.axis_index("dp"), lax.axis_index("tensor")
    n_all = n_dp * n_tensor
    me = my_dp * n_tensor + my_tensor
    order = sorted(range(count), key=lambda job: ("in", "out", "all", "rs", "ag").index(kinds[job]))
    flowing = [job for job in order if kinds[job] == "in"]

    def wide_peer(step):
        peer = lax.rem(me + step, n_all)
        return peer // n_tensor, lax.rem(peer, n_tensor)

    def narrow_peer(step):
        return lax.rem(my_dp + step, n_dp), my_tensor

    barrier = pltpu.get_barrier_semaphore()
    wide = any(kind in WIDE + ("in",) for kind in kinds)
    total = n_all if wide else n_dp
    pick = wide_peer if wide else narrow_peer

    @pl.loop(1, total)
    def greet(step):
        peer_dp, peer_tensor = pick(step)
        pl.semaphore_signal(
            barrier, inc=1, device_id={"dp": peer_dp, "tensor": peer_tensor}, device_id_type=MESH
        )

    pl.semaphore_wait(barrier, total - 1)

    def block(job, peer_dp, peer_tensor):
        kind = kinds[job]
        if kind in ("ag", "all"):
            return sources[job]
        if kind == "out":
            return sources[job].at[peer_dp, peer_tensor]
        return sources[job].at[peer_dp]

    def place(job):
        if kinds[job] in WIDE + ("in",):
            return targets[job].at[my_dp, my_tensor]
        return targets[job].at[my_dp]

    def steps(job):
        return n_all if kinds[job] in WIDE else n_dp

    def remote(job, step):
        peer_dp, peer_tensor = wide_peer(step) if kinds[job] in WIDE else narrow_peer(step)
        return pltpu.make_async_remote_copy(
            src_ref=block(job, peer_dp, peer_tensor),
            dst_ref=place(job),
            send_sem=send_sem.at[job, step],
            recv_sem=recv_sem.at[job, step],
            device_id={"dp": peer_dp, "tensor": peer_tensor},
            device_id_type=MESH,
        )

    def local(job):
        return pltpu.make_async_copy(block(job, my_dp, my_tensor), place(job), local_sem.at[job])

    def hop(job, step, source, move):
        owner = lax.rem(my_dp + n_dp - step, n_dp)
        sems = up_sem if move == 1 else down_sem
        return pltpu.make_async_remote_copy(
            src_ref=targets[job].at[owner, source],
            dst_ref=targets[job].at[owner, source],
            send_sem=sems.at[0, job, step, source],
            recv_sem=sems.at[1, job, step, source],
            device_id={"dp": my_dp, "tensor": lax.rem(my_tensor + move + n_tensor, n_tensor)},
            device_id_type=MESH,
        )

    for job in order:

        @pl.loop(1, steps(job))
        def send(step, job=job):
            remote(job, step).start()

    for job in order:
        local(job).start()
    for job in order:
        local(job).wait()

    def pass_on(job, step, source):
        @pl.when((source <= my_tensor) & (my_tensor < n_tensor - 1))
        def up():
            hop(job, step, source, 1).start()

        @pl.when((source >= my_tensor) & (my_tensor > 0))
        def down():
            hop(job, step, source, -1).start()

    for job in flowing:
        pass_on(job, 0, my_tensor)

        @pl.loop(1, n_dp)
        def first(step, job=job):
            remote(job, step).wait_recv()
            pass_on(job, step, my_tensor)

    for job in flowing:

        @pl.loop(1, n_tensor)
        def onward(distance, job=job):
            below, above = my_tensor - distance, my_tensor + distance

            @pl.loop(0, n_dp)
            def piece(step):
                @pl.when(below >= 0)
                def from_below():
                    hop(job, step, below, 1).wait_recv()
                    pass_on(job, step, below)

                @pl.when(above < n_tensor)
                def from_above():
                    hop(job, step, above, -1).wait_recv()
                    pass_on(job, step, above)

    for job in flowing:

        @pl.loop(1, n_dp)
        def sent(step, job=job):
            remote(job, step).wait_send()

        @pl.loop(0, n_tensor)
        def handed(source, job=job):
            @pl.loop(0, n_dp)
            def piece(step):
                @pl.when((source <= my_tensor) & (my_tensor < n_tensor - 1))
                def up():
                    hop(job, step, source, 1).wait_send()

                @pl.when((source >= my_tensor) & (my_tensor > 0))
                def down():
                    hop(job, step, source, -1).wait_send()

    for job in order:
        if job not in flowing:

            @pl.loop(1, steps(job))
            def finish(step, job=job):
                remote(job, step).wait()


def exchange(collective_id, *jobs):
    n_dp, n_tensor = lax.axis_size("dp"), lax.axis_size("tensor")
    kinds = tuple(kind for kind, _ in jobs)
    arrays = [value for _, value in jobs]
    shapes = []
    for kind, value in jobs:
        lead = {
            "in": (n_dp, n_tensor) + value.shape[1:],
            "out": value.shape,
            "all": (n_dp, n_tensor) + value.shape,
            "rs": value.shape,
            "ag": (n_dp,) + value.shape,
        }[kind]
        shapes.append(jax.ShapeDtypeStruct(lead, value.dtype))
    count = len(jobs)
    most = n_dp * n_tensor
    return pl.pallas_call(
        functools.partial(exchange_kernel, kinds, n_dp, n_tensor),
        out_shape=shapes,
        in_specs=[pl.BlockSpec(memory_space=pl.ANY)] * count,
        out_specs=[pl.BlockSpec(memory_space=pl.ANY)] * count,
        scratch_shapes=[
            pltpu.SemaphoreType.DMA((count, most)),
            pltpu.SemaphoreType.DMA((count, most)),
            pltpu.SemaphoreType.DMA((2, count, n_dp, n_tensor)),
            pltpu.SemaphoreType.DMA((2, count, n_dp, n_tensor)),
            pltpu.SemaphoreType.DMA((count,)),
        ],
        compiler_params=pltpu.CompilerParams(
            collective_id=collective_id, has_side_effects=True
        ),
        name="exchange_" + "_".join(kinds),
    )(*arrays)


def from_behind(value, axis, steps):
    count = lax.axis_size(axis)
    pairs = [(source, (source + steps) % count) for source in range(count)]
    return lax.ppermute(value, axis, pairs)


def rope_tables(segments):
    count_rows = segments.shape[1]
    row_index = jnp.arange(count_rows, dtype=jnp.int32)
    allowed = (segments[:, :, None] == segments[:, None, :]) & (
        row_index[:, None] >= row_index[None, :]
    )[None]
    allowed = allowed.astype(F32)
    positions = jnp.sum(allowed, axis=2) - 1.0
    halfway = HD // 2
    frequency = jnp.exp(jnp.arange(halfway, dtype=F32) * (-2.0 * math.log(ROPE_BASE) / HD))
    angles = positions[:, :, None] * frequency
    cosine, sine = jnp.cos(angles), jnp.sin(angles)
    return (
        jnp.concatenate([cosine, cosine], axis=2),
        jnp.concatenate([-sine, sine], axis=2),
        allowed,
    )


def dot(left, right, contract):
    return lax.dot_general(left, right, (contract, ((), ())), preferred_element_type=F32)


ROWS_COLUMNS, COLUMNS_COLUMNS, ROWS_ROWS = ((1,), (0,)), ((1,), (1,)), ((0,), (0,))


def total(pieces, first):
    value = pieces[0, :, first : first + HD].astype(F32)
    for index in range(1, pieces.shape[0]):
        value = value + pieces[index, :, first : first + HD].astype(F32)
    return value


def turn(value, cosine, sine):
    return value * cosine + pltpu.roll(value, HD // 2, 1) * sine


def softmax(query, key, allowed):
    scores = dot(query, key, COLUMNS_COLUMNS) * (1.0 / math.sqrt(HD))
    exponents = jnp.exp(jnp.where(allowed > 0.5, scores, -1e30))
    return exponents / jnp.sum(exponents, axis=1, keepdims=True)


def attention_kernel(widths, pieces, cosine, sine, allowed, mixed):
    query_width, key_width = widths
    group = query_width // key_width
    cos, sin, keep = cosine[...], sine[...], allowed[...]
    for key_head in range(key_width // HD):
        key = turn(total(pieces, query_width + key_head * HD), cos, sin).astype(BF16)
        value = total(pieces, query_width + key_width + key_head * HD).astype(BF16)
        for head in range(key_head * group, (key_head + 1) * group):
            query = turn(total(pieces, head * HD), cos, sin).astype(BF16)
            probs = softmax(query, key, keep).astype(BF16)
            mixed[:, head * HD : (head + 1) * HD] = dot(probs, value, ROWS_COLUMNS).astype(BF16)


def attention_gradient_kernel(widths, pieces, grads, cosine, sine, allowed, gradient):
    query_width, key_width = widths
    group = query_width // key_width
    cos, sin, keep = cosine[...], sine[...], allowed[...]
    for key_head in range(key_width // HD):
        key_at = query_width + key_head * HD
        value_at = key_at + key_width
        key = turn(total(pieces, key_at), cos, sin).astype(BF16)
        value = total(pieces, value_at).astype(BF16)
        key_grad = jnp.zeros(key.shape, F32)
        value_grad = jnp.zeros(key.shape, F32)
        for head in range(key_head * group, (key_head + 1) * group):
            query = turn(total(pieces, head * HD), cos, sin).astype(BF16)
            mixed_grad = total(grads, head * HD).astype(BF16)
            probs = softmax(query, key, keep)
            value_grad = value_grad + dot(probs.astype(BF16), mixed_grad, ROWS_ROWS)
            probs_grad = dot(mixed_grad, value, COLUMNS_COLUMNS).astype(BF16).astype(F32)
            mean = jnp.sum(probs_grad * probs, axis=1, keepdims=True)
            scores_grad = (probs * (probs_grad - mean) * (1.0 / math.sqrt(HD))).astype(BF16)
            query_grad = dot(scores_grad, key, ROWS_COLUMNS).astype(BF16).astype(F32)
            gradient[:, head * HD : (head + 1) * HD] = turn(query_grad, cos, -sin).astype(BF16)
            key_grad = key_grad + dot(scores_grad, query, ROWS_ROWS)
        key_grad = key_grad.astype(BF16).astype(F32)
        gradient[:, key_at : key_at + HD] = turn(key_grad, cos, -sin).astype(BF16)
        gradient[:, value_at : value_at + HD] = value_grad.astype(BF16)


def in_vmem(kernel, widths, out_width, *operands):
    count_rows = operands[0].shape[1]
    return pl.pallas_call(
        functools.partial(kernel, widths),
        out_shape=jax.ShapeDtypeStruct((count_rows, out_width), BF16),
        in_specs=[pl.BlockSpec(memory_space=pltpu.VMEM)] * len(operands),
        out_specs=pl.BlockSpec(memory_space=pltpu.VMEM),
        compiler_params=pltpu.CompilerParams(vmem_limit_bytes=32 * 1024 * 1024),
    )(*operands)


def normalise(rows, gain_vector):
    variance = jnp.mean(rows * rows, axis=1, keepdims=True)
    return rows * lax.rsqrt(variance + 1e-06) * gain_vector


def pick_span(table, span):
    return lax.dynamic_index_in_dim(table, span, 0, keepdims=False)


def dot_t(left, right):
    return lax.dot_general(left, right, (((1,), (1,)), ((), ())), preferred_element_type=F32)


def per_device(
    fwd_state, bwd_state, stash, gains, w_query, w_key, w_value, w_out, fwd_segments, bwd_segments
):
    n_dp, n_tensor = lax.axis_size("dp"), lax.axis_size("tensor")
    phase_count = lax.axis_size("section")
    phase_index = lax.axis_index("section")
    own_rows, model_width = fwd_state.shape[1:]
    part = model_width // n_dp
    replica_rows = own_rows * n_tensor
    all_rows = replica_rows * n_dp
    widths = (w_query.shape[3], w_key.shape[3])

    def columns(rows):
        return rows.reshape(own_rows, n_dp, part).transpose(1, 0, 2)

    def project(normed, span):
        normed = normed.reshape(all_rows, part)
        pieces = [
            jnp.dot(normed, pick_span(weight[0], span), preferred_element_type=F32).astype(BF16)
            for weight in (w_query, w_key, w_value)
        ]
        return jnp.concatenate(pieces, axis=1).reshape(n_dp, replica_rows, -1)

    def to_owners(term):
        return term.astype(BF16).reshape(n_dp, n_tensor, own_rows, part)

    def rows_of(pieces):
        return jnp.sum(pieces.astype(F32), axis=1).transpose(1, 0, 2).reshape(own_rows, model_width)

    gains32 = gains[0].astype(F32)
    my_part = lax.dynamic_slice_in_dim(gains32, lax.axis_index("dp") * part, part, axis=1)
    stash32 = stash[0].astype(F32)
    fwd_spans = [jnp.where(phase_index < tick, 1, 0).astype(jnp.int32) for tick in range(TICKS)]
    bwd_spans = [
        jnp.where(phase_index > phase_count - 1 - tick, 0, 1).astype(jnp.int32)
        for tick in range(TICKS)
    ]
    rows_ids = [
        pick_span(fwd_segments[:, 0], (phase_index - tick) % phase_count) for tick in range(TICKS)
    ] + [pick_span(bwd_segments[:, 0], (phase_index + tick) % phase_count) for tick in range(TICKS)]
    tables = rope_tables(jnp.stack(rows_ids))

    def attention(projected, tick):
        return in_vmem(
            attention_kernel, widths, widths[0], projected, *[table[tick] for table in tables]
        )

    def forward_in(state_rows, tick):
        gain = pick_span(gains32, fwd_spans[tick])
        return columns(normalise(state_rows.astype(F32), gain).astype(BF16))

    def stash_in(tick):
        gain = pick_span(gains32, bwd_spans[tick])
        return columns(normalise(stash32[tick], gain).astype(BF16))

    def forward_out(mixed, tick):
        mixed = mixed.reshape(all_rows, -1)
        return to_owners(
            jnp.dot(mixed, pick_span(w_out[0], fwd_spans[tick]), preferred_element_type=F32)
        )

    def mixed_gradient(grad, tick):
        grad = grad.reshape(all_rows, part)
        return (
            dot_t(grad, pick_span(w_out[0], bwd_spans[tick]))
            .astype(BF16)
            .reshape(n_dp, replica_rows, -1)
        )

    def attention_gradient(projected, mixed_grad, tick):
        return in_vmem(
            attention_gradient_kernel,
            widths,
            widths[0] + 2 * widths[1],
            projected,
            mixed_grad,
            *[table[TICKS + tick] for table in tables],
        )

    def normed_gradient(gradient, normed, tick):
        gradient = gradient.reshape(all_rows, -1)
        span = bwd_spans[tick]
        query_width, key_width = widths
        term = (
            dot_t(gradient[:, :query_width], pick_span(w_query[0], span))
            + dot_t(gradient[:, query_width : query_width + key_width], pick_span(w_key[0], span))
            + dot_t(gradient[:, query_width + key_width :], pick_span(w_value[0], span))
        )
        gain_term = jnp.sum(term * normed.reshape(all_rows, part).astype(F32), axis=0)
        gain_term = gain_term / pick_span(my_part, span)
        return to_owners(term), gain_term.reshape(-1, 128)

    def returned_rows(grad_rows, pieces, tick):
        gain = pick_span(gains32, bwd_spans[tick])
        _, pull = jax.vjp(lambda rows: normalise(rows, gain), stash32[tick])
        return (grad_rows.astype(F32) + pull(rows_of(pieces))[0]).astype(BF16)

    span_ids = jnp.arange(2, dtype=jnp.int32)

    def gain_rows(pieces, tick):
        gain = jnp.sum(pieces, axis=1).reshape(model_width)
        chosen = (span_ids == bwd_spans[tick]).astype(F32)
        return chosen[:, None] * gain[None, :]

    state_rows, grad_rows = fwd_state[0], bwd_state[0]
    (stash0,) = exchange(0, ("in", stash_in(0)))
    grad, bwd_proj = exchange(
        1, ("in", columns(grad_rows)), ("rs", project(stash0, bwd_spans[0]))
    )
    state, mixed_grad = exchange(
        2, ("in", forward_in(state_rows, 0)), ("rs", mixed_gradient(grad, 0))
    )
    gradient = attention_gradient(bwd_proj, mixed_grad, 0)
    stash1, fwd_proj, gradient = exchange(
        3, ("in", stash_in(1)), ("rs", project(state, fwd_spans[0])), ("ag", gradient)
    )
    term, gain_term = normed_gradient(gradient, stash0, 0)
    mixed = attention(fwd_proj, 0)
    bwd_pieces, gain0, mixed = exchange(4, ("out", term), ("all", gain_term), ("ag", mixed))
    grad_rows = from_behind(returned_rows(grad_rows, bwd_pieces, 0), "section", -1)
    fwd_pieces, grad, bwd_proj = exchange(
        5,
        ("out", forward_out(mixed, 0)),
        ("in", columns(grad_rows)),
        ("rs", project(stash1, bwd_spans[1])),
    )
    advanced = (state_rows.astype(F32) + rows_of(fwd_pieces)).astype(BF16)
    state_rows = from_behind(advanced, "section", 1)
    state, mixed_grad = exchange(
        6, ("in", forward_in(state_rows, 1)), ("rs", mixed_gradient(grad, 1))
    )
    gradient = attention_gradient(bwd_proj, mixed_grad, 1)
    fwd_proj, gradient = exchange(
        7, ("rs", project(state, fwd_spans[1])), ("ag", gradient)
    )
    term, gain_term = normed_gradient(gradient, stash1, 1)
    mixed = attention(fwd_proj, 1)
    bwd_pieces, gain1, mixed = exchange(8, ("out", term), ("all", gain_term), ("ag", mixed))
    grad_rows = from_behind(returned_rows(grad_rows, bwd_pieces, 1), "section", -1)
    (fwd_pieces,) = exchange(9, ("out", forward_out(mixed, 1)))
    advanced = (state_rows.astype(F32) + rows_of(fwd_pieces)).astype(BF16)
    state_rows = from_behind(advanced, "section", 1)
    gain_total = gain_rows(gain0, 0) + gain_rows(gain1, 1)
    return (state_rows[None], grad_rows[None], gain_total[None])


def solution(mesh):
    in_specs = (
        P("section", ("dp", "tensor"), None),
        P("section", ("dp", "tensor"), None),
        P("section", None, ("dp", "tensor"), None),
        P("section", None, None),
        P("section", None, "dp", "tensor"),
        P("section", None, "dp", "tensor"),
        P("section", None, "dp", "tensor"),
        P("section", None, "tensor", "dp"),
        P(None, "dp", None),
        P(None, "dp", None),
    )
    out_specs = (
        P("section", ("dp", "tensor"), None),
        P("section", ("dp", "tensor"), None),
        P("section", None, None),
    )
    return jax.shard_map(
        per_device, mesh=mesh, in_specs=in_specs, out_specs=out_specs, check_vma=False
    )
```

profile of v0, /device:TPU:0, one launch (start us, length us, event | category | flops | bytes accessed | tf_op | source)
XLA Modules:
  0.0 464.1 jit_solution(1513218464322172793)
XLA Ops:
  9.7 29.1 %exchange_in.1 = bf16[4,4,32,1024]{3,2,1,0:T(8,128)(2,1)} custom-call(bf16[4,32,1024]{2,1,0:T(8,128)(2,1)} %fusion.104.refs_0_), custom_call_target="tpu_custom_call" | custom-call | tf_op jit(solution)/shard_map/exchange_in/pallas_call | solution.py:182
  42.2 2.9 fusion.30
  46.4 35.7 %exchange_in_rs.3 = (bf16[4,4,32,1024]{3,2,1,0:T(8,128)(2,1)}, bf16[4,128,1536]{2,1,0:T(8,128)(2,1)}) custom-call(bf16[4,32,1024]{2,1,0:T(8,128)(2,1)} %bitcast.256, bf16[4,128,1536]{2,1,0:T(8,128)(2,1)} %bitcast.233), custom_call_target="tpu_custom_call" | custom-call | tf_op jit(solution)/shard_map/exchange_in_rs/pallas_call | solution.py:182
  82.1 4.2 fusion.33
  87.3 33.2 %exchange_in_rs.4 = (bf16[4,4,32,1024]{3,2,1,0:T(8,128)(2,1)}, bf16[4,128,1024]{2,1,0:T(8,128)(2,1)}) custom-call(bf16[4,32,1024]{2,1,0:T(8,128)(2,1)} %fusion.103.refs_0_, bf16[4,128,1024]{2,1,0:T(8,128)(2,1)} %bitcast.255), custom_call_target="tpu_custom_call" | custom-call | tf_op jit(solution)/shard_map/exchange_in_rs/pallas_call | solution.py:182
  125.4 3.9 fusion.36
  137.2 2.6 shard_map.121.refs_2_
  140.5 47.9 %exchange_in_rs_ag.1 = (bf16[4,4,32,1024]{3,2,1,0:T(8,128)(2,1)}, bf16[4,128,1536]{2,1,0:T(8,128)(2,1)}, bf16[4,128,1536]{2,1,0:T(8,128)(2,1)}) custom-call(bf16[4,32,1024]{2,1,0:T(8,128)(2,1)} %fusion.102.refs_0_, bf16[4,128,1536]{2,1,0:T(8,128)(2,1)} %bitcast.232, bf16[128,1536]{1,0:T(8,128)(2,1)} %copy-done.5), custom_call_target="tpu_custom_call" | custom-call | tf_op jit(solution)/shard_map/exchange_in_rs_ag/pallas_call | solution.py:182
  188.5 4.6 fusion.16
  193.1 2.7 fusion.75
  195.8 4.3 multiply_reduce_fusion.1
  203.8 29.7 %exchange_out_all_ag.2 = (bf16[4,4,32,1024]{3,2,1,0:T(8,128)(2,1)}, f32[4,4,8,128]{3,2,1,0:T(8,128)}, bf16[4,128,1024]{2,1,0:T(8,128)(2,1)}) custom-call(bf16[4,4,32,1024]{3,2,1,0:T(8,128)(2,1)} %bitcast.243, f32[8,128]{1,0:T(8,128)} %bitcast_divide_fusion.1.refs_1_, bf16[128,1024]{1,0:T(8,128)(2,1)} %copy-done.9), custom_call_target="tpu_custom_call" | custom-call | tf_op jit(solution)/shard_map/exchange_out_all_ag/pallas_call | solution.py:182
  243.1 2.6 pad_maximum_fusion.2
  246.5 45.5 %exchange_out_in_rs.1 = (bf16[4,4,32,1024]{3,2,1,0:T(8,128)(2,1)}, bf16[4,4,32,1024]{3,2,1,0:T(8,128)(2,1)}, bf16[4,128,1536]{2,1,0:T(8,128)(2,1)}) custom-call(bf16[4,4,32,1024]{3,2,1,0:T(8,128)(2,1)} %bitcast.261, bf16[4,32,1024]{2,1,0:T(8,128)(2,1)} %bitcast.262, bf16[4,128,1536]{2,1,0:T(8,128)(2,1)} %bitcast.235), custom_call_target="tpu_custom_call" | custom-call | tf_op jit(solution)/shard_map/exchange_out_in_rs/pallas_call | solution.py:182
  293.8 3.9 fusion.45
  298.7 34.0 %exchange_in_rs.5 = (bf16[4,4,32,1024]{3,2,1,0:T(8,128)(2,1)}, bf16[4,128,1024]{2,1,0:T(8,128)(2,1)}) custom-call(bf16[4,32,1024]{2,1,0:T(8,128)(2,1)} %bitcast.257, bf16[4,128,1024]{2,1,0:T(8,128)(2,1)} %bitcast.254), custom_call_target="tpu_custom_call" | custom-call | tf_op jit(solution)/shard_map/exchange_in_rs/pallas_call | solution.py:182
  336.2 2.9 fusion.48
  341.4 2.6 shard_map.123.refs_1_
  344.7 39.0 %exchange_rs_ag.1 = (bf16[4,128,1536]{2,1,0:T(8,128)(2,1)}, bf16[4,128,1536]{2,1,0:T(8,128)(2,1)}) custom-call(bf16[4,128,1536]{2,1,0:T(8,128)(2,1)} %bitcast.234, bf16[128,1536]{1,0:T(8,128)(2,1)} %copy-done.6), custom_call_target="tpu_custom_call" | custom-call | tf_op jit(solution)/shard_map/exchange_rs_ag/pallas_call | solution.py:182
  383.7 3.3 fusion.6
  388.5 2.7 multiply_reduce_fusion
  394.8 32.5 %exchange_out_all_ag.3 = (bf16[4,4,32,1024]{3,2,1,0:T(8,128)(2,1)}, f32[4,4,8,128]{3,2,1,0:T(8,128)}, bf16[4,128,1024]{2,1,0:T(8,128)(2,1)}) custom-call(bf16[4,4,32,1024]{3,2,1,0:T(8,128)(2,1)} %bitcast.244, f32[8,128]{1,0:T(8,128)} %bitcast_divide_fusion.refs_1_, bf16[128,1024]{1,0:T(8,128)(2,1)} %copy-done.10), custom_call_target="tpu_custom_call" | custom-call | tf_op jit(solution)/shard_map/exchange_out_all_ag/pallas_call | solution.py:182
  427.3 4.2 fusion.51
  431.4 26.8 %exchange_out.1 = bf16[4,4,32,1024]{3,2,1,0:T(8,128)(2,1)} custom-call(bf16[4,4,32,1024]{3,2,1,0:T(8,128)(2,1)} %bitcast.259), custom_call_target="tpu_custom_call" | custom-call | tf_op jit(solution)/shard_map/exchange_out/pallas_call | solution.py:182
  (183 shorter events, 62.0 us)
Async XLA Ops:
  0.6 38.1 %copy-start = (bf16[1,2,1024,256]{3,2,1,0:T(8,128)(2,1)S(1)}, bf16[1,2,1024,256]{3,2,1,0:T(8,128)(2,1)}, u32[]{:S(2)}) copy-start(bf16[1,2,1024,256]{3,2,1,0:T(8,128)(2,1)} %param.16) | copy-start | bytes 3145732
  3.0 5.1 %copy-start.11 = (f32[1,2,32,4096]{3,2,1,0:T(8,128)}, f32[1,2,32,4096]{3,2,1,0:T(8,128)S(1)}, u32[]{:S(2)}) copy-start(f32[1,2,32,4096]{3,2,1,0:T(8,128)S(1)} %convert_element_type.152) | copy-start | bytes 3145732
  3.9 34.9 %copy-start.37 = (f32[32]{0:T(128)}, f32[32]{0:T(128)S(1)}, u32[]{:S(2)}) copy-start(f32[32]{0:T(128)S(1)} %get-tuple-element.44) | copy-start | bytes 388
  3.9 34.9 %copy-start.39 = (f32[32]{0:T(128)}, f32[32]{0:T(128)S(1)}, u32[]{:S(2)}) copy-start(f32[32]{0:T(128)S(1)} %get-tuple-element.43) | copy-start | bytes 388
  8.1 32.4 %copy-start.25 = (bf16[1,2,1024,256]{3,2,1,0:T(8,128)(2,1)S(1)}, bf16[1,2,1024,256]{3,2,1,0:T(8,128)(2,1)}, u32[]{:S(2)}) copy-start(bf16[1,2,1024,256]{3,2,1,0:T(8,128)(2,1)} %param.15) | copy-start | bytes 3145732
  8.7 33.6 %copy-start.35 = (f32[32]{0:T(128)}, f32[32]{0:T(128)S(1)}, u32[]{:S(2)}) copy-start(f32[32]{0:T(128)S(1)} %get-tuple-element.83) | copy-start | bytes 388
  86.3 36.7 %copy-start.26 = (bf16[1,2,1024,256]{3,2,1,0:T(8,128)(2,1)S(1)}, bf16[1,2,1024,256]{3,2,1,0:T(8,128)(2,1)}, u32[]{:S(2)}) copy-start(bf16[1,2,1024,256]{3,2,1,0:T(8,128)(2,1)} %param.15) | copy-start | bytes 3145732
  120.5 4.8 %copy-start.47 = (bf16[4,4,32,1024]{3,2,1,0:T(8,128)(2,1)S(1)}, bf16[4,4,32,1024]{3,2,1,0:T(8,128)(2,1)}, u32[]{:S(2)}) copy-start(bf16[4,4,32,1024]{3,2,1,0:T(8,128)(2,1)} %get-tuple-element.24) | copy-start | bytes 3145732
  125.4 4.0 copy-start.41
  125.4 4.0 copy-start.42
  125.4 5.1 %copy-start.16 = (f32[1,1,32,4096]{3,2,1,0:T(8,128)S(1)}, f32[1,1,32,4096]{3,2,1,0:T(8,128)}, u32[]{:S(2)}) copy-start(f32[1,1,32,4096]{3,2,1,0:T(8,128)} %get-tuple-element.58) | copy-start | bytes 1572868
  130.8 4.1 copy-start.19
  133.1 4.1 copy-start.1
  133.1 4.1 copy-start.7
  188.5 4.6 copy-start.27
  195.8 5.0 %copy-start.3 = (bf16[4,128,1536]{2,1,0:T(8,128)(2,1)S(1)}, bf16[4,128,1536]{2,1,0:T(8,128)(2,1)}, u32[]{:S(2)}) copy-start(bf16[4,128,1536]{2,1,0:T(8,128)(2,1)} %get-tuple-element.28.pieces) | copy-start | bytes 4718596
  203.8 31.3 %copy-start.12 = (f32[1,2,32,4096]{3,2,1,0:T(8,128)S(1)}, f32[1,2,32,4096]{3,2,1,0:T(8,128)}, u32[]{:S(2)}) copy-start(f32[1,2,32,4096]{3,2,1,0:T(8,128)} %copy-done.11) | copy-start | bytes 3145732
  236.2 9.5 %collective-permute-start = (bf16[32,4096]{1,0:T(8,128)(2,1)}, bf16[32,4096]{1,0:T(8,128)(2,1)S(1)}, u32[]{:S(2)}, u32[]{:S(2)}) collective-permute-start(bf16[32,4096]{1,0:T(8,128)(2,1)} %fusion.57), channel_id=1, source_target_pairs={{0,4},{4,0},{1,5},{5,1},{2,6},{6,2},{3,7},{7,3},{8,12},{12,8},{9,1... | collective-permute-start | bytes 786440 | tf_op jit(solution)/shard_map/ppermute | solution.py:204
  245.7 46.3 %copy-start.23 = (bf16[32,4096]{1,0:T(8,128)(2,1)}, bf16[32,4096]{1,0:T(8,128)(2,1)S(1)}, u32[]{:S(2)}) copy-start(bf16[32,4096]{1,0:T(8,128)(2,1)S(1)} %collective-permute-done) | copy-start | bytes 786436
  293.7 4.0 collective-permute-start.1
  293.7 4.1 copy-start.32
  332.7 3.6 copy-start.48
  460.0 2.0 collective-permute-start.2
  461.1 1.6 collective-permute-start.3
  (29 other events, 54.7 us)
where the time goes:
time: 465 us; the launch traced here: 464 us
  Pallas kernels  363 us (78%)
  matrix products  59 us (13%)
  other arithmetic  23.1 us (5%)
  local copies, waits for them, and re-layouts  16.5 us (4%)
    pallas_call x10, Pallas kernels, exchange(): pl.pallas_call(functools.partial(exchange_kernel, kinds, n_dp, n_tensor),...  353 us
    dot_general x8, matrix products, dot_t(): lax.dot_general(left, right, (((1,), (1,)), ((), ())), preferred_element_...  27.2 us
    dot_general x12, matrix products, project(): jnp.dot(normed, pick_span(weight[0], span), preferred_element_type=F32)  25.4 us
    pallas_call x4, Pallas kernels, in_vmem(): pl.pallas_call(functools.partial(kernel, widths), out_shape=jax.ShapeDtyp...  9.57 us
  transfers between devices with their start and end apart: 4, of which 1 were waited for; matrix products, arithmetic and copies ran while one was open for 3% of the time, Pallas kernels for 0%

commit v1 on v0

--- a/solution.py
+++ b/solution.py
@@ -416,43 +416,45 @@
         return chosen[:, None] * gain[None, :]
 
     state_rows, grad_rows = fwd_state[0], bwd_state[0]
-    (stash0,) = exchange(0, ("in", stash_in(0)))
-    grad, bwd_proj = exchange(
-        1, ("in", columns(grad_rows)), ("rs", project(stash0, bwd_spans[0]))
-    )
-    state, mixed_grad = exchange(
-        2, ("in", forward_in(state_rows, 0)), ("rs", mixed_gradient(grad, 0))
+    stash0, state = exchange(0, ("in", stash_in(0)), ("in", forward_in(state_rows, 0)))
+    grad, bwd_proj, fwd_proj = exchange(
+        1,
+        ("in", columns(grad_rows)),
+        ("rs", project(stash0, bwd_spans[0])),
+        ("rs", project(state, fwd_spans[0])),
+    )
+    stash1, mixed_grad, mixed = exchange(
+        2,
+        ("in", stash_in(1)),
+        ("rs", mixed_gradient(grad, 0)),
+        ("ag", attention(fwd_proj, 0)),
     )
     gradient = attention_gradient(bwd_proj, mixed_grad, 0)
-    stash1, fwd_proj, gradient = exchange(
-        3, ("in", stash_in(1)), ("rs", project(state, fwd_spans[0])), ("ag", gradient)
-    )
-    term, gain_term = normed_gradient(gradient, stash0, 0)
-    mixed = attention(fwd_proj, 0)
-    bwd_pieces, gain0, mixed = exchange(4, ("out", term), ("all", gain_term), ("ag", mixed))
-    grad_rows = from_behind(returned_rows(grad_rows, bwd_pieces, 0), "section", -1)
-    fwd_pieces, grad, bwd_proj = exchange(
-        5,
-        ("out", forward_out(mixed, 0)),
-        ("in", columns(grad_rows)),
-        ("rs", project(stash1, bwd_spans[1])),
-    )
+    fwd_pieces, gradient = exchange(3, ("out", forward_out(mixed, 0)), ("ag", gradient))
     advanced = (state_rows.astype(F32) + rows_of(fwd_pieces)).astype(BF16)
     state_rows = from_behind(advanced, "section", 1)
-    state, mixed_grad = exchange(
-        6, ("in", forward_in(state_rows, 1)), ("rs", mixed_gradient(grad, 1))
+    term, gain_term = normed_gradient(gradient, stash0, 0)
+    bwd_pieces, gain0, state, bwd_proj = exchange(
+        4,
+        ("out", term),
+        ("all", gain_term),
+        ("in", forward_in(state_rows, 1)),
+        ("rs", project(stash1, bwd_spans[1])),
+    )
+    grad_rows = from_behind(returned_rows(grad_rows, bwd_pieces, 0), "section", -1)
+    grad, fwd_proj = exchange(
+        5, ("in", columns(grad_rows)), ("rs", project(state, fwd_spans[1]))
+    )
+    mixed_grad, mixed = exchange(
+        6, ("rs", mixed_gradient(grad, 1)), ("ag", attention(fwd_proj, 1))
     )
     gradient = attention_gradient(bwd_proj, mixed_grad, 1)
-    fwd_proj, gradient = exchange(
-        7, ("rs", project(state, fwd_spans[1])), ("ag", gradient)
-    )
-    term, gain_term = normed_gradient(gradient, stash1, 1)
-    mixed = attention(fwd_proj, 1)
-    bwd_pieces, gain1, mixed = exchange(8, ("out", term), ("all", gain_term), ("ag", mixed))
-    grad_rows = from_behind(returned_rows(grad_rows, bwd_pieces, 1), "section", -1)
-    (fwd_pieces,) = exchange(9, ("out", forward_out(mixed, 1)))
+    fwd_pieces, gradient = exchange(7, ("out", forward_out(mixed, 1)), ("ag", gradient))
     advanced = (state_rows.astype(F32) + rows_of(fwd_pieces)).astype(BF16)
     state_rows = from_behind(advanced, "section", 1)
+    term, gain_term = normed_gradient(gradient, stash1, 1)
+    bwd_pieces, gain1 = exchange(8, ("out", term), ("all", gain_term))
+    grad_rows = from_behind(returned_rows(grad_rows, bwd_pieces, 1), "section", -1)
     gain_total = gain_rows(gain0, 0) + gain_rows(gain1, 1)
     return (state_rows[None], grad_rows[None], gain_total[None])
 

time: 465 us -> 469 us (level)
    pallas_call x10 -> x9, Pallas kernels: 353 us -> 352 us  [exchange(): pl.pallas_call(functools.partial(exchange_kernel, kinds, n_dp, n_tensor),...]
  transfers between devices with their start and end apart: 4 -> 4, of which waited for: 1 -> 1; matrix products, arithmetic and copies ran while one was open for 3% -> 7% of each run, Pallas kernels for 0% -> 7%
where the time goes in v1:
time: 469 us; the launch traced here: 468 us
  Pallas kernels  362 us (77%)
  matrix products  61.5 us (13%)
  other arithmetic  25 us (5%)
  local copies, waits for them, and re-layouts  17.6 us (4%)
    pallas_call x9, Pallas kernels, exchange(): pl.pallas_call(functools.partial(exchange_kernel, kinds, n_dp, n_tensor),...  352 us
    dot_general x12, matrix products, project(): jnp.dot(normed, pick_span(weight[0], span), preferred_element_type=F32)  26.7 us
    dot_general x8, matrix products, dot_t(): lax.dot_general(left, right, (((1,), (1,)), ((), ())), preferred_element_...  26.3 us
    pallas_call x4, Pallas kernels, in_vmem(): pl.pallas_call(functools.partial(kernel, widths), out_shape=jax.ShapeDtyp...  9.58 us
  transfers between devices with their start and end apart: 4, of which 1 were waited for; matrix products, arithmetic and copies ran while one was open for 7% of the time, Pallas kernels for 7%

profile of v1, /device:TPU:0, one launch (start us, length us, event | category | flops | bytes accessed | tf_op | source)
XLA Modules:
  0.0 467.8 jit_solution(13961887884311102401)
XLA Ops:
  9.1 49.0 %exchange_in_in.1 = (bf16[4,4,32,1024]{3,2,1,0:T(8,128)(2,1)}, bf16[4,4,32,1024]{3,2,1,0:T(8,128)(2,1)}) custom-call(bf16[4,32,1024]{2,1,0:T(8,128)(2,1)} %fusion.103.refs_0_, bf16[4,32,1024]{2,1,0:T(8,128)(2,1)} %fusion.104.refs_1_), custom_call_target="tpu_custom_call" | custom-call | tf_op jit(solution)/shard_map/exchange_in_in/pallas_call | solution.py:182
  60.6 2.6 convolution_convert_fusion.7
  79.9 48.4 %exchange_in_rs_rs.1 = (bf16[4,4,32,1024]{3,2,1,0:T(8,128)(2,1)}, bf16[4,128,1536]{2,1,0:T(8,128)(2,1)}, bf16[4,128,1536]{2,1,0:T(8,128)(2,1)}) custom-call(bf16[4,32,1024]{2,1,0:T(8,128)(2,1)} %bitcast.261, bf16[4,128,1536]{2,1,0:T(8,128)(2,1)} %bitcast.234, bf16[4,128,1536]{2,1,0:T(8,128)(2,1)} %bitcast.235), custom_call_target="tpu_custom_call" | custom-call | tf_op jit(solution)/shard_map/exchange_in_rs_rs/pallas_call | solution.py:182
  128.4 4.3 fusion.36
  137.0 42.4 %exchange_in_rs_ag.1 = (bf16[4,4,32,1024]{3,2,1,0:T(8,128)(2,1)}, bf16[4,128,1024]{2,1,0:T(8,128)(2,1)}, bf16[4,128,1024]{2,1,0:T(8,128)(2,1)}) custom-call(bf16[4,32,1024]{2,1,0:T(8,128)(2,1)} %fusion.102.refs_0_, bf16[4,128,1024]{2,1,0:T(8,128)(2,1)} %bitcast.256, bf16[128,1024]{1,0:T(8,128)(2,1)} %copy-done.10), custom_call_target="tpu_custom_call" | custom-call | tf_op jit(solution)/shard_map/exchange_in_rs_ag/pallas_call | solution.py:182
  179.3 4.3 fusion.39
  183.6 2.6 shard_map.122.refs_1_
  187.0 32.4 %exchange_out_ag.2 = (bf16[4,4,32,1024]{3,2,1,0:T(8,128)(2,1)}, bf16[4,128,1536]{2,1,0:T(8,128)(2,1)}) custom-call(bf16[4,4,32,1024]{3,2,1,0:T(8,128)(2,1)} %bitcast.259, bf16[128,1536]{1,0:T(8,128)(2,1)} %copy-done.3), custom_call_target="tpu_custom_call" | custom-call | tf_op jit(solution)/shard_map/exchange_out_ag/pallas_call | solution.py:182
  221.8 4.3 fusion.16
  231.5 3.8 fusion.42
  235.8 4.3 multiply_reduce_fusion.1
  241.3 2.5 pad_maximum_fusion.2
  244.8 47.7 %exchange_out_all_in_rs.1 = (bf16[4,4,32,1024]{3,2,1,0:T(8,128)(2,1)}, f32[4,4,8,128]{3,2,1,0:T(8,128)}, bf16[4,4,32,1024]{3,2,1,0:T(8,128)(2,1)}, bf16[4,128,1536]{2,1,0:T(8,128)(2,1)}) custom-call(bf16[4,4,32,1024]{3,2,1,0:T(8,128)(2,1)} %bitcast.240, f32[8,128]{1,0:T(8,128)} %bitcast_divide_fusion.1.refs_1_, bf16[4,32,1024]{2,1,0:T(8,128)(2,1)} %bitcast.262, ...), custom_call_target="tpu_custom_call" | custom-call | tf_op jit(solution)/shard_map/exchange_out_all_in_rs/pallas_call | solution.py:182
  296.2 3.9 fusion.45
  303.4 2.5 pad_maximum_fusion.3
  306.6 38.2 %exchange_in_rs.1 = (bf16[4,4,32,1024]{3,2,1,0:T(8,128)(2,1)}, bf16[4,128,1536]{2,1,0:T(8,128)(2,1)}) custom-call(bf16[4,32,1024]{2,1,0:T(8,128)(2,1)} %bitcast.255, bf16[4,128,1536]{2,1,0:T(8,128)(2,1)} %bitcast.232), custom_call_target="tpu_custom_call" | custom-call | tf_op jit(solution)/shard_map/exchange_in_rs/pallas_call | solution.py:182
  344.8 4.3 fusion.48
  352.1 27.8 %exchange_rs_ag.1 = (bf16[4,128,1024]{2,1,0:T(8,128)(2,1)}, bf16[4,128,1024]{2,1,0:T(8,128)(2,1)}) custom-call(bf16[4,128,1024]{2,1,0:T(8,128)(2,1)} %bitcast.254, bf16[128,1024]{1,0:T(8,128)(2,1)} %copy-done.9), custom_call_target="tpu_custom_call" | custom-call | tf_op jit(solution)/shard_map/exchange_rs_ag/pallas_call | solution.py:182
  379.9 4.3 fusion.51
  384.2 2.6 shard_map.124.refs_1_
  387.5 34.0 %exchange_out_ag.3 = (bf16[4,4,32,1024]{3,2,1,0:T(8,128)(2,1)}, bf16[4,128,1536]{2,1,0:T(8,128)(2,1)}) custom-call(bf16[4,4,32,1024]{3,2,1,0:T(8,128)(2,1)} %bitcast.258, bf16[128,1536]{1,0:T(8,128)(2,1)} %copy-done.4), custom_call_target="tpu_custom_call" | custom-call | tf_op jit(solution)/shard_map/exchange_out_ag/pallas_call | solution.py:182
  421.5 3.3 fusion.6
  427.6 2.6 multiply_reduce_fusion
  430.8 32.0 %exchange_out_all.1 = (bf16[4,4,32,1024]{3,2,1,0:T(8,128)(2,1)}, f32[4,4,8,128]{3,2,1,0:T(8,128)}) custom-call(bf16[4,4,32,1024]{3,2,1,0:T(8,128)(2,1)} %bitcast.241, f32[8,128]{1,0:T(8,128)} %bitcast_divide_fusion.refs_1_), custom_call_target="tpu_custom_call" | custom-call | tf_op jit(solution)/shard_map/exchange_out_all/pallas_call | solution.py:182
  (186 shorter events, 62.5 us)
Async XLA Ops:
  0.6 57.5 %copy-start = (bf16[1,2,1024,256]{3,2,1,0:T(8,128)(2,1)S(1)}, bf16[1,2,1024,256]{3,2,1,0:T(8,128)(2,1)}, u32[]{:S(2)}) copy-start(bf16[1,2,1024,256]{3,2,1,0:T(8,128)(2,1)} %param.16) | copy-start | bytes 3145732
  7.0 56.1 %copy-start.40 = (f32[32]{0:T(128)}, f32[32]{0:T(128)S(1)}, u32[]{:S(2)}) copy-start(f32[32]{0:T(128)S(1)} %get-tuple-element.48) | copy-start | bytes 388
  7.0 56.1 %copy-start.42 = (f32[32]{0:T(128)}, f32[32]{0:T(128)S(1)}, u32[]{:S(2)}) copy-start(f32[32]{0:T(128)S(1)} %get-tuple-element.47) | copy-start | bytes 388
  7.1 56.1 %copy-start.38 = (f32[32]{0:T(128)}, f32[32]{0:T(128)S(1)}, u32[]{:S(2)}) copy-start(f32[32]{0:T(128)S(1)} %get-tuple-element.89) | copy-start | bytes 388
  7.1 125.7 %copy-start.36 = (f32[32]{0:T(128)}, f32[32]{0:T(128)S(1)}, u32[]{:S(2)}) copy-start(f32[32]{0:T(128)S(1)} %get-tuple-element.88) | copy-start | bytes 388
  9.1 51.5 %copy-start.25 = (bf16[1,2,1024,256]{3,2,1,0:T(8,128)(2,1)S(1)}, bf16[1,2,1024,256]{3,2,1,0:T(8,128)(2,1)}, u32[]{:S(2)}) copy-start(bf16[1,2,1024,256]{3,2,1,0:T(8,128)(2,1)} %param.15) | copy-start | bytes 3145732
  58.1 5.1 %copy-start.50 = (bf16[4,4,32,1024]{3,2,1,0:T(8,128)(2,1)S(1)}, bf16[4,4,32,1024]{3,2,1,0:T(8,128)(2,1)}, u32[]{:S(2)}) copy-start(bf16[4,4,32,1024]{3,2,1,0:T(8,128)(2,1)} %get-tuple-element.26) | copy-start | bytes 3145732
  60.6 4.9 %copy-start.48 = (bf16[1,2,1024,1024]{3,2,1,0:T(8,128)(2,1)S(1)}, bf16[1,2,1024,1024]{3,2,1,0:T(8,128)(2,1)}, u32[]{:S(2)}) copy-start(bf16[1,2,1024,1024]{3,2,1,0:T(8,128)(2,1)} %param.14) | copy-start | bytes 12582916
  67.8 4.7 copy-start.23
  72.6 3.7 copy-start.19
  128.3 4.3 copy-start.22
  128.3 4.4 copy-start.13
  179.3 4.3 copy-start.2
  179.3 4.3 copy-start.8
  221.8 22.0 %collective-permute-start = (bf16[32,4096]{1,0:T(8,128)(2,1)}, bf16[32,4096]{1,0:T(8,128)(2,1)S(1)}, u32[]{:S(2)}, u32[]{:S(2)}) collective-permute-start(bf16[32,4096]{1,0:T(8,128)(2,1)} %fusion.83), channel_id=1, source_target_pairs={{0,4},{4,0},{1,5},{5,1},{2,6},{6,2},{3,7},{7,3},{8,12},{12,8},{9,1... | collective-permute-start | bytes 786440 | tf_op jit(solution)/shard_map/ppermute | solution.py:204
  221.8 4.3 copy-start.26
  292.6 3.6 copy-start.49
  296.2 3.9 copy-start.20
  302.0 3.9 collective-permute-start.1
  344.8 4.3 copy-start.6
  379.9 4.3 copy-start.1
  379.9 4.3 copy-start.7
  426.7 39.2 %collective-permute-start.2 = (bf16[32,4096]{1,0:T(8,128)(2,1)S(1)}, bf16[32,4096]{1,0:T(8,128)(2,1)S(1)}, u32[]{:S(2)}, u32[]{:S(2)}) collective-permute-start(bf16[32,4096]{1,0:T(8,128)(2,1)S(1)} %fusion.59), channel_id=1, source_target_pairs={{0,4},{4,0},{1,5},{5,1},{2,6},{6,2},{3,7},{7,3},{8,12},{12,8},{9,1... | collective-permute-start | bytes 786440 | tf_op jit(solution)/shard_map/ppermute | solution.py:204
  464.8 1.6 collective-permute-start.3
  (31 other events, 57.9 us)
